TPU v7x, 32 devices: a whole 2x2x4 slice. The times are simulated.
32 devices in a mesh: ens: 2 (over x), row: 16 (over z, y, core).
Axes of the slice: x: 2, y: 2, z: 4, core: 2. Of those that a mesh axis runs over, the one named last changes fastest.
Arguments:
- jacobian: float32 [32768, 256], P(('ens', 'row')), parts along dimension 0, may hold values from -40 to 40
- residuals: float32 [32768, 128], P(('ens', 'row')), parts along dimension 0, may hold values from -6 to 6
Outputs:
- ortho_basis: float32 [32768, 256], P(('ens', 'row')), parts along dimension 0
- factor: float32 [512, 256], P('ens'), parts along dimension 0
- update: float32 [512, 128], P('ens'), parts along dimension 0
There are 2 independent parts, one for each index of `ens`. A program takes and returns all parts, laid end to end along the dimension named above; each array names one. Nothing has to cross between parts.
All inputs are finite; a program needn't handle non-finite values.
Results may differ from a plain program's by a relative error of at most 0.0003.
Values sent between devices are 32-bit elements; how exact they have to be, the bound alone decides.
A program may use at most 64 MiB of HBM per device.

v0:
```python
import jax
import jax.numpy as jnp
from jax import lax
from jax.sharding import PartitionSpec as P


def cross_product(left, right):
    contract = (((0,), (0,)), ((), ()))
    return lax.dot_general(
        left, right, contract, precision=lax.Precision.HIGHEST, preferred_element_type=jnp.float32
    )


def cholesky_upper(gram_matrix):
    width = gram_matrix.shape[0]
    positions = jnp.arange(width, dtype=jnp.int32)

    def column_step(column, carry):
        remaining, upper = carry
        onehot = (positions == column).astype(jnp.float32)
        column_values = jnp.sum(remaining * onehot[None, :], axis=1)
        pivot_value = jnp.sqrt(jnp.sum(column_values * onehot))
        new_row = column_values / pivot_value * (positions >= column).astype(jnp.float32)
        upper = upper + onehot[:, None] * new_row[None, :]
        remaining = remaining - new_row[:, None] * new_row[None, :]
        return (remaining, upper)

    start = (gram_matrix, jnp.zeros_like(gram_matrix))
    return lax.fori_loop(0, width, column_step, start)[1]


def invert_upper(upper):
    width = upper.shape[0]
    positions = jnp.arange(width, dtype=jnp.int32)

    def row_step(counter, inverse):
        current = width - 1 - counter
        onehot = (positions == current).astype(jnp.float32)
        upper_row = jnp.sum(upper * onehot[:, None], axis=0)
        diagonal_entry = jnp.sum(upper_row * onehot)
        product = jnp.dot(
            upper_row, inverse, precision=lax.Precision.HIGHEST, preferred_element_type=jnp.float32
        )
        new_row = (onehot - product) / diagonal_entry
        return inverse + onehot[:, None] * new_row[None, :]

    return lax.fori_loop(0, width, row_step, jnp.zeros_like(upper))


def shards(jacobian, residuals):
    precise = lax.Precision.HIGHEST
    rows_all = jacobian.shape[0] * lax.axis_size("row")
    gram_matrix = cross_product(jacobian, jacobian) / rows_all
    data_total = None
    data_terms = cross_product(jacobian, residuals)
    summed_gram, data_total = lax.psum((gram_matrix, data_terms), "row")
    factor = cholesky_upper(summed_gram)
    inverse = invert_upper(factor)
    ortho_basis = jnp.dot(jacobian, inverse, precision=precise, preferred_element_type=jnp.float32)
    root_rows = jnp.sqrt(jnp.float32(rows_all))
    projected = cross_product(inverse, data_total) / root_rows
    update = jnp.dot(inverse, projected, precision=precise, preferred_element_type=jnp.float32)
    return (ortho_basis, factor, update)


def solution(mesh):
    return jax.shard_map(
        shards,
        mesh=mesh,
        in_specs=(P(("ens", "row"), None), P(("ens", "row"), None)),
        out_specs=(P(("ens", "row"), None), P("ens", None), P("ens", None)),
        check_vma=False,
    )
```

profile of v0, /device:TPU:0, one launch (start us, length us, event | category | flops | bytes accessed | tf_op | source)
XLA Modules:
  0.0 1418.8 jit_solution(2986073664823571487)
XLA Ops:
  7.2 1.2 copy-done
  8.4 2.5 convolution_multiply_fusion
  10.9 2.5 fusion.15
  13.4 93.5 %all-reduce.3.cloned.1.call-done = (f32[256,256]{1,0:T(8,128)}, f32[256,128]{1,0:T(8,128)}) async-done(((f32[256,256]{1,0:T(8,128)}, f32[256,128]{1,0:T(8,128)}), (f32[256,256]{1,0:T(8,128)}, f32[256,128]{1,0:T(8,128)})) %all-reduce.3.cloned.1.call-update) | async-done | bytes 393232 | tf_op jit(solution)/shard_map/psum | solution.py:56
  107.0 849.4 %while.32 = (s32[]{:T(128)}, f32[256,256]{1,0:T(8,128)}, f32[256,256]{1,0:T(8,128)S(1)}, s32[]{:T(128)}, s32[]{:T(128)}) while((s32[]{:T(128)}, f32[256,256]{1,0:T(8,128)}, f32[256,256]{1,0:T(8,128)S(1)}, s32[]{:T(128)}, s32[]{:T(128)}) %tuple.70), condition=%wide.region_4.5_spmd.clone.clone, body=%wide.region_1.4_spmd.clone.clone.sunk | while | flops 460546 | bytes 3416227 | solution.py:29
  107.0 1.1 multiply_reduce_fusion.5
  110.3 1.1 multiply_reduce_fusion.5
  116.9 1.1 multiply_reduce_fusion.5
  120.2 1.1 multiply_reduce_fusion.5
  123.6 1.1 multiply_reduce_fusion.5
  130.2 1.1 multiply_reduce_fusion.5
  133.5 1.1 multiply_reduce_fusion.5
  143.5 1.1 multiply_reduce_fusion.5
  146.8 1.1 multiply_reduce_fusion.5
  153.4 1.1 multiply_reduce_fusion.5
  156.7 1.1 multiply_reduce_fusion.5
  160.1 1.1 multiply_reduce_fusion.5
  166.7 1.1 multiply_reduce_fusion.5
  170.0 1.1 multiply_reduce_fusion.5
  173.3 1.1 multiply_reduce_fusion.5
  180.0 1.1 multiply_reduce_fusion.5
  183.3 1.1 multiply_reduce_fusion.5
  186.6 1.1 multiply_reduce_fusion.5
  193.2 1.1 multiply_reduce_fusion.5
  196.5 1.1 multiply_reduce_fusion.5
  206.5 1.1 multiply_reduce_fusion.5
  209.8 1.1 multiply_reduce_fusion.5
  216.5 1.1 multiply_reduce_fusion.5
  219.8 1.1 multiply_reduce_fusion.5
  956.3 450.8 %while.31 = (s32[]{:T(128)}, f32[256,256]{1,0:T(8,128)S(1)}, f32[256,256]{1,0:T(8,128)S(1)}, s32[]{:T(128)}, s32[]{:T(128)}, /*index=5*/s32[]{:T(128)}) while((s32[]{:T(128)}, f32[256,256]{1,0:T(8,128)S(1)}, f32[256,256]{1,0:T(8,128)S(1)}, s32[]{:T(128)}, s32[]{:T(128)}, /*index=5*/s32[]{:T(128)}) %tuple.73), condition=%wide.region_8.9_spmd.clone, body=%wide.region_5.8_spmd.clone.sunk | while | flops 1181699 | bytes 1058936 | solution.py:47
  1407.2 1.9 convolution_bitcast_fusion
  1410.7 1.3 copy.5
  (3829 shorter events, 1077.0 us)
Async XLA Ops:
  7.2 3.8 copy-start.4
  7.2 99.8 %all-reduce.3.cloned.1.call-start = ((), (), s32[]{:S(2)}) async-start(), calls=%async_computation | async-start | bytes 786432 | tf_op jit(solution)/shard_map/psum | solution.py:56
  107.0 2.5 copy-start.1
  110.3 2.5 copy-start.1
  113.6 2.5 copy-start.1
  116.9 2.5 copy-start.1
  120.2 2.5 copy-start.1
  123.5 2.5 copy-start.1
  126.9 2.5 copy-start.1
  130.2 2.5 copy-start.1
  133.5 2.5 copy-start.1
  136.8 2.5 copy-start.1
  140.1 2.5 copy-start.1
  143.5 2.5 copy-start.1
  150.1 2.5 copy-start.1
  153.4 2.5 copy-start.1
  156.7 2.5 copy-start.1
  160.0 2.5 copy-start.1
  163.4 2.5 copy-start.1
  166.7 2.5 copy-start.1
  170.0 2.5 copy-start.1
  173.3 2.5 copy-start.1
  176.6 2.5 copy-start.1
  180.0 2.5 copy-start.1
  183.3 2.5 copy-start.1
  186.6 2.5 copy-start.1
  189.9 2.5 copy-start.1
  193.2 2.5 copy-start.1
  196.5 2.5 copy-start.1
  199.9 2.5 copy-start.1
  203.2 2.5 copy-start.1
  206.5 2.5 copy-start.1
  (485 other events, 736.4 us)
Sparse Core Ops, SparseCore 0:
  13.5 93.3 all-reduce.2
where the time goes:
time: 1430 us; the launch traced here: 1420 us
  other arithmetic  878 us (61%)
  loops' own time  198 us (14%)
  local copies, waits for them, and re-layouts  179 us (13%)
  waiting for transfers between devices  93.5 us (7%)
  matrix products  57 us (4%)
    reduce_sum x256, other arithmetic, column_step(): column_values = jnp.sum(remaining * onehot[None, :], axis=1)  289 us
    another operation x1, loops' own time, cholesky_upper(): return lax.fori_loop(0, width, column_step, start)[1]  187 us
    div x256, other arithmetic, row_step(): new_row = (onehot - product) / diagonal_entry  177 us
    while x1024, local copies, waits for them, and re-layouts  176 us
    reduce_sum x256, other arithmetic, row_step(): diagonal_entry = jnp.sum(upper_row * onehot)  155 us
    reduce_sum x256, other arithmetic, column_step(): pivot_value = jnp.sqrt(jnp.sum(column_values * onehot))  155 us
    psum x1, waiting for transfers between devices, shards(): summed_gram, data_total = lax.psum((gram_matrix, data_terms), 'row')  93.5 us
    dot_general x256, matrix products, row_step(): jnp.dot(upper_row, inverse, precision=lax.Precision.HIGHEST, preferred_el...  48.5 us
  transfers between devices with their start and end apart: 1, of which 1 were waited for; matrix products, arithmetic and copies ran while one was open for 0% of the time, Pallas kernels for 0%

commit v1 on v0

v1 whole, which is shorter than its diff:
```python
import jax, jax.numpy as jnp, functools
from jax import lax
from jax.experimental import pallas as pl
from jax.experimental.pallas import tpu as pltpu
HI = lax.Precision.HIGHEST
F32 = jnp.float32

def recip(p):
    return 1.0 / p

def factor_rows(x, extra, first, width):
    nb = x.shape[0]
    diag = []
    mults = []
    rows = [x[8 * i:8 * i + 8] for i in range(nb // 8)]
    ext = [extra[8 * i:8 * i + 8] for i in range(nb // 8)]
    sub = lax.broadcasted_iota(jnp.int32, (8, 128), 0)
    pivots = []
    for p in range(nb // 8):
        cols = []
        for l in range(8):
            c = first + 8 * p + l
            cols.append([jnp.broadcast_to(rows[i][:, c:c + 1], (8, 128)) for i in range(p, nb // 8)])
        pv = jnp.ones((8, 128), F32)
        for j in range(8):
            piv = jnp.broadcast_to(cols[j][0][j:j + 1], (8, 128))
            pv = jnp.where(sub == j, piv, pv)
            r = recip(piv)
            f = [cj * r for cj in cols[j]]
            f[0] = jnp.where(sub > j, f[0], 0.0)
            for l in range(j + 1, 8):
                e = jnp.broadcast_to(cols[l][0][j:j + 1], (8, 128))
                cols[l] = [cl - fi * e for cl, fi in zip(cols[l], f)]
            n = rows[0].shape[1]
            xr = jnp.broadcast_to(rows[p][j:j + 1], (8, n))
            er = jnp.broadcast_to(ext[p][j:j + 1], (8, 128))
            for q, fi in enumerate(f):
                rows[p + q] = rows[p + q] - jnp.concatenate([fi] * (n // 128), axis=1) * xr
                ext[p + q] = ext[p + q] - fi * er
        pivots.append(pv)
    out_r, out_e = [], []
    for i in range(nb // 8):
        s = lax.rsqrt(pivots[i])
        n = rows[0].shape[1]
        out_r.append(rows[i] * jnp.concatenate([s] * (n // 128), axis=1))
        out_e.append(ext[i] * s)
    return jnp.concatenate(out_r, 0), jnp.concatenate(out_e, 0)

def dot(a, b, dims, prec=HI):
    return lax.dot_general(a, b, (dims, ((), ())), precision=prec, preferred_element_type=F32)

def eliminate(blocks, nb):
    n = blocks[0].shape[1]
    count = n // nb
    lane = lax.broadcasted_iota(jnp.int32, (nb, n), 1)
    lane1 = lax.broadcasted_iota(jnp.int32, (nb, 128), 1)
    sub1 = lax.broadcasted_iota(jnp.int32, (nb, 128), 0)
    upper, low = [], []
    for k in range(count):
        off = (k * nb) % 128
        eye = (lane1 == sub1 + off).astype(F32)
        x, e = factor_rows(blocks[k], eye, k * nb, n)
        mine = (lane >= k * nb) & (lane < (k + 1) * nb)
        wide = jnp.concatenate([e] * (n // 128), axis=1)
        t = jnp.where(mine, wide, x)
        urow = lane1[:, :1] * 0 + lax.broadcasted_iota(jnp.int32, (nb, n), 0) + k * nb
        upper.append(jnp.where(lane >= urow, x, 0.0))
        low.append(jnp.where(lane < (k + 1) * nb, t, 0.0))
        if k + 1 < count:
            for i in range(k + 1, count):
                lhs = x[:, i * nb:(i + 1) * nb]
                upd = dot(lhs, t, ((0,), (0,)))
                blocks[i] = jnp.where(mine, 0.0, blocks[i]) - upd
    return upper, low


def factor_kernel(gram_ref, upper_ref, low_ref):
    nb = 32
    n = gram_ref.shape[0]
    blocks = [gram_ref[i * nb:(i + 1) * nb, :] for i in range(n // nb)]
    upper, low = eliminate(blocks, nb)
    for i in range(n // nb):
        upper_ref[i * nb:(i + 1) * nb, :] = upper[i]
        low_ref[i * nb:(i + 1) * nb, :] = low[i]


def shards(jacobian, residuals):
    rows_all = jacobian.shape[0] * lax.axis_size("row")
    gram = dot(jacobian, jacobian, ((0,), (0,))) / rows_all
    data = dot(jacobian, residuals, ((0,), (0,)))
    gram, data = lax.psum((gram, data), "row")
    shape = jax.ShapeDtypeStruct(gram.shape, F32)
    factor, low = pl.pallas_call(factor_kernel, out_shape=(shape, shape),
        compiler_params=pltpu.CompilerParams(vmem_limit_bytes=32 * 1024 * 1024))(gram)
    basis = dot(jacobian, low, ((1,), (1,)))
    projected = dot(low, data, ((1,), (0,))) / jnp.sqrt(jnp.float32(rows_all))
    update = dot(low, projected, ((0,), (0,)))
    return (basis, factor, update)


def solution(mesh):
    from jax.sharding import PartitionSpec as P
    return jax.shard_map(
        shards,
        mesh=mesh,
        in_specs=(P(("ens", "row"), None), P(("ens", "row"), None)),
        out_specs=(P(("ens", "row"), None), P("ens", None), P("ens", None)),
        check_vma=False,
    )
```

time: 1430 us -> 128 us (0.09)
  other arithmetic: 878 us -> 0 us
  loops' own time: 198 us -> 0 us
  local copies, waits for them, and re-layouts: 179 us -> 3.43 us
  matrix products: 57 us -> 7.68 us
    reduce_sum x1024 -> x0, other arithmetic: 629 us -> none  [the longest x256 289 us: column_step(): column_values = jnp.sum(remaining * onehot[None, :], axis=1)]
    another operation x2 -> x0, loops' own time: 198 us -> none  [the longest x1 187 us: cholesky_upper(): return lax.fori_loop(0, width, column_step, start)[1]]
    div x256 -> x0, other arithmetic: 177 us -> none  [row_step(): new_row = (onehot - product) / diagonal_entry]
    while x1024 -> x0, local copies, waits for them, and re-layouts: 176 us -> none
    add x512 -> x0, other arithmetic: 69 us -> none  [the longest x256 40.3 us: column_step(): upper = upper + onehot[:, None] * new_row[None, :]]
    dot_general x261 -> x5, matrix products: 57 us -> 7.68 us  [dot(): lax.dot_general(a, b, (dims, ((), ())), precision=prec, preferred_element...]
where the time goes in v1:
time: 128 us
  waiting for transfers between devices  93.5 us (73%)
  between operations  14.1 us (11%)
  Pallas kernels  9.05 us (7%)
  matrix products  7.68 us (6%)
  local copies, waits for them, and re-layouts  3.43 us (3%)
    psum x1, waiting for transfers between devices, shards(): gram, data = lax.psum((gram, data), 'row')  93.5 us
    pallas_call x1, Pallas kernels, shards(): pl.pallas_call(factor_kernel, out_shape=(shape, shape), compiler_params=p...  9.05 us
    dot_general x5, matrix products, dot(): lax.dot_general(a, b, (dims, ((), ())), precision=prec, preferred_element...  7.68 us
    unnamed x9, local copies, waits for them, and re-layouts  3.43 us
  transfers between devices with their start and end apart: 1, of which 1 were waited for; matrix products, arithmetic and copies ran while one was open for 0% of the time, Pallas kernels for 0%

profile of v1, /device:TPU:0, one launch (start us, length us, event | category | flops | bytes accessed | tf_op | source)
XLA Modules:
  0.0 127.8 jit_solution(11752162239343072674)
XLA Ops:
  7.2 0.0 copy-start
  7.2 0.0 copy-start.2
  7.2 0.0 all-reduce.3.cloned.1.call-start
  7.2 1.2 copy-done
  8.4 2.5 %convolution_multiply_fusion = f32[256,256]{1,0:T(8,128)} fusion(f32[1024,256]{1,0:T(8,128)S(1)} %copy-done), kind=kOutput, calls=%fused_computation.1 | convolution fusion | flops 805371904 | bytes 1310720 | tf_op jit(solution)/shard_map/dot_general | solution.py:50
  10.9 0.0 copy-done.2
  10.9 2.5 %fusion = f32[256,128]{1,0:T(8,128)} fusion(f32[1024,256]{1,0:T(8,128)S(1)} %copy-done, f32[1024,128]{1,0:T(8,128)S(1)} %copy-done.2), kind=kOutput, calls=%fused_computation.3 | convolution fusion | flops 402653184 | bytes 1703936 | tf_op jit(solution)/shard_map/dot_general | solution.py:50
  13.4 0.0 all-reduce.3.cloned.1.call-update
  13.4 93.5 %all-reduce.3.cloned.1.call-done = (f32[256,256]{1,0:T(8,128)}, f32[256,128]{1,0:T(8,128)}) async-done(((f32[256,256]{1,0:T(8,128)}, f32[256,128]{1,0:T(8,128)}), (f32[256,256]{1,0:T(8,128)}, f32[256,128]{1,0:T(8,128)})) %all-reduce.3.cloned.1.call-update) | async-done | bytes 393232 | tf_op jit(solution)/shard_map/psum | solution.py:91
  107.0 0.0 copy-start.1
  107.0 0.9 copy-done.1
  107.9 9.0 %shard_map.49 = (f32[256,256]{1,0:T(8,128)}, f32[256,256]{1,0:T(8,128)S(1)}) custom-call(f32[256,256]{1,0:T(8,128)S(1)} %copy-done.1), custom_call_target="tpu_custom_call" | custom-call | tf_op jit(solution)/shard_map/pallas_call | solution.py:93
  117.0 0.0 copy-start.3
  117.0 1.0 convolution_bitcast_fusion
  118.0 0.0 copy-done.3
  118.0 0.4 convolution_multiply_fusion.1
  118.4 1.3 fusion.1
  119.7 1.3 %copy.5 = f32[1024,256]{1,0:T(8,128)} copy(f32[1024,256]{0,1:T(8,128)S(1)} %convolution_bitcast_fusion) | data formatting | bytes 2097152
Async XLA Ops:
  7.2 1.2 copy-start
  7.2 3.8 %copy-start.2 = (f32[1024,128]{1,0:T(8,128)S(1)}, f32[1024,128]{1,0:T(8,128)}, u32[]{:S(2)}) copy-start(f32[1024,128]{1,0:T(8,128)} %param.3) | copy-start | bytes 1572868
  7.2 99.8 %all-reduce.3.cloned.1.call-start = ((), (), s32[]{:S(2)}) async-start(), calls=%async_computation | async-start | bytes 786432 | tf_op jit(solution)/shard_map/psum | solution.py:91
  107.0 0.9 copy-start.1
  117.0 1.1 copy-start.3
Sparse Core Ops, SparseCore 0:
  13.5 93.3 all-reduce.2

commit v2 on v1

--- a/solution.py
+++ b/solution.py
@@ -1,12 +1,13 @@
-import jax, jax.numpy as jnp, functools
+import functools
+import jax
+import jax.numpy as jnp
 from jax import lax
 from jax.experimental import pallas as pl
 from jax.experimental.pallas import tpu as pltpu
+from jax.sharding import PartitionSpec as P
+
 HI = lax.Precision.HIGHEST
 F32 = jnp.float32
-
-def recip(p):
-    return 1.0 / p
 
 def factor_rows(x, extra, first, width):
     nb = x.shape[0]
@@ -25,7 +26,7 @@
         for j in range(8):
             piv = jnp.broadcast_to(cols[j][0][j:j + 1], (8, 128))
             pv = jnp.where(sub == j, piv, pv)
-            r = recip(piv)
+            r = 1.0 / piv
             f = [cj * r for cj in cols[j]]
             f[0] = jnp.where(sub > j, f[0], 0.0)
             for l in range(j + 1, 8):
@@ -49,6 +50,19 @@
 def dot(a, b, dims, prec=HI):
     return lax.dot_general(a, b, (dims, ((), ())), precision=prec, preferred_element_type=F32)
 
+def split3(x):
+    high = x.astype(jnp.bfloat16)
+    rest = x - high.astype(F32)
+    middle = rest.astype(jnp.bfloat16)
+    return high, middle, (rest - middle.astype(F32)).astype(jnp.bfloat16)
+
+
+def stacked_product(left, right):
+    a, b, c = split3(left)
+    d, e, f = split3(right)
+    return dot(jnp.concatenate([a, a, b, b, a, c], 0), jnp.concatenate([d, e, d, e, f, d], 0), ((0,), (0,)), None)
+
+
 def eliminate(blocks, nb):
     n = blocks[0].shape[1]
     count = n // nb
@@ -67,39 +81,160 @@
         upper.append(jnp.where(lane >= urow, x, 0.0))
         low.append(jnp.where(lane < (k + 1) * nb, t, 0.0))
         if k + 1 < count:
+            update = stacked_product(x, t)
             for i in range(k + 1, count):
-                lhs = x[:, i * nb:(i + 1) * nb]
-                upd = dot(lhs, t, ((0,), (0,)))
-                blocks[i] = jnp.where(mine, 0.0, blocks[i]) - upd
+                blocks[i] = jnp.where(mine, 0.0, blocks[i]) - update[i * nb:(i + 1) * nb]
     return upper, low
 
 
-def factor_kernel(gram_ref, upper_ref, low_ref):
+def gram_kernel(levels, rows_all, jac_ref, res_ref, gram_ref, data_ref, part, total, *scratch):
+    recvs, sums = scratch[:len(levels)], scratch[len(levels):2 * len(levels)]
+    rs_send, rs_recv, ag_send, ag_recv = scratch[2 * len(levels):]
+    me = lax.axis_index("row")
+    places = []
+    stride = 1
+    for size in levels:
+        places.append((lax.rem(me // stride, size), stride, size))
+        stride *= size
+
+    def peer(level, step):
+        place, stride, size = places[level]
+        other = lax.rem(place + step, size)
+        return other, me + (other - place) * stride
+
+    barrier = pltpu.get_barrier_semaphore()
+    for level, size in enumerate(levels):
+        for step in range(1, size):
+            pl.semaphore_signal(barrier, inc=1, device_id={"row": peer(level, step)[1]}, device_id_type=pl.DeviceIdType.MESH)
+
+    n = jac_ref.shape[1]
+    half = n // 2
+    res = res_ref[...]
+    first = dot(jac_ref[:, :half], jnp.concatenate([jac_ref[...], res], 1), ((0,), (0,)))
+    second = dot(jac_ref[:, half:], jnp.concatenate([jac_ref[:, half:], res], 1), ((0,), (0,)))
+    tiles = [first[:, :half], first[:, half:n], second[:, :half], first[:, n:], second[:, half:]]
+    for i, tile in enumerate(tiles):
+        part[i * half:(i + 1) * half] = tile
+    if part.shape[0] > 5 * half:
+        part[5 * half:] = jnp.zeros((part.shape[0] - 5 * half, half), F32)
+    pl.semaphore_wait(barrier, sum(size - 1 for size in levels))
+
+    source = part
+    slot = 0
+    for level, size in enumerate(levels):
+        seg = source.shape[0] // size
+        place = places[level][0]
+        copies = []
+        for step in range(1, size):
+            other, device = peer(level, step)
+            copies.append(pltpu.make_async_remote_copy(
+                src_ref=source.at[pl.ds(pl.multiple_of(other * seg, 8), seg)],
+                dst_ref=recvs[level].at[step - 1],
+                send_sem=rs_send.at[slot], recv_sem=rs_recv.at[slot],
+                device_id={"row": device}, device_id_type=pl.DeviceIdType.MESH))
+            copies[-1].start()
+            slot += 1
+        value = source[pl.ds(pl.multiple_of(place * seg, 8), seg)]
+        for step in range(1, size):
+            copies[step - 1].wait_recv()
+            value = value + recvs[level][step - 1]
+        sums[level][...] = value
+        for copy in copies:
+            copy.wait_send()
+        source = sums[level]
+
+    starts = []
+    start = 0
+    seg = part.shape[0]
+    for place, _, size in places:
+        seg //= size
+        start = start + place * seg
+        starts.append((start, seg))
+    total[pl.ds(pl.multiple_of(start, 8), seg)] = source[...]
+    slot = 0
+    for level in reversed(range(len(levels))):
+        start, seg = starts[level]
+        mine = total.at[pl.ds(pl.multiple_of(start, 8), seg)]
+        copies = []
+        for step in range(1, levels[level]):
+            copies.append(pltpu.make_async_remote_copy(
+                src_ref=mine, dst_ref=mine,
+                send_sem=ag_send.at[slot], recv_sem=ag_recv.at[slot],
+                device_id={"row": peer(level, step)[1]}, device_id_type=pl.DeviceIdType.MESH))
+            copies[-1].start()
+            slot += 1
+        for copy in copies:
+            copy.wait()
+    scale = 1.0 / rows_all
+    gram_ref[:half, :half] = total[:half] * scale
+    gram_ref[:half, half:] = total[half:n] * scale
+    gram_ref[half:, :half] = jnp.zeros((half, half), F32)
+    gram_ref[half:, half:] = total[n:n + half] * scale
+    data_ref[...] = total[n + half:2 * n + half]
+
+
+def solve_kernel(rows_all, gram_ref, data_ref, jac_ref, basis_ref, upper_ref, update_ref, jac, basis, in_sem, out_sem):
+    load = pltpu.make_async_copy(jac_ref, jac, in_sem)
+    load.start()
     nb = 32
     n = gram_ref.shape[0]
     blocks = [gram_ref[i * nb:(i + 1) * nb, :] for i in range(n // nb)]
     upper, low = eliminate(blocks, nb)
     for i in range(n // nb):
         upper_ref[i * nb:(i + 1) * nb, :] = upper[i]
-        low_ref[i * nb:(i + 1) * nb, :] = low[i]
+    low = jnp.concatenate(low, 0)
+    load.wait()
+    chunk = jac.shape[0] // 4
+    stores = []
+    for i in range(4):
+        basis[i * chunk:(i + 1) * chunk] = dot(jac[i * chunk:(i + 1) * chunk], low, ((1,), (1,)))
+        stores.append(pltpu.make_async_copy(
+            basis.at[pl.ds(i * chunk, chunk)], basis_ref.at[pl.ds(i * chunk, chunk)], out_sem.at[i]))
+        stores[-1].start()
+    projected = dot(low, data_ref[...], ((1,), (0,))) * (1.0 / rows_all ** 0.5)
+    update_ref[...] = dot(low, projected, ((0,), (0,)))
+    for store in stores:
+        store.wait()
 
 
 def shards(jacobian, residuals):
-    rows_all = jacobian.shape[0] * lax.axis_size("row")
-    gram = dot(jacobian, jacobian, ((0,), (0,))) / rows_all
-    data = dot(jacobian, residuals, ((0,), (0,)))
-    gram, data = lax.psum((gram, data), "row")
-    shape = jax.ShapeDtypeStruct(gram.shape, F32)
-    factor, low = pl.pallas_call(factor_kernel, out_shape=(shape, shape),
-        compiler_params=pltpu.CompilerParams(vmem_limit_bytes=32 * 1024 * 1024))(gram)
-    basis = dot(jacobian, low, ((1,), (1,)))
-    projected = dot(low, data, ((1,), (0,))) / jnp.sqrt(jnp.float32(rows_all))
-    update = dot(low, projected, ((0,), (0,)))
-    return (basis, factor, update)
+    devices = lax.axis_size("row")
+    rows, n = jacobian.shape
+    rhs = residuals.shape[1]
+    half = n // 2
+    rows_all = rows * devices
+    levels = (2, devices // 2)
+    unit = 8 * devices
+    length = -(-5 * half // unit) * unit
+    recvs, sums = [], []
+    seg = length
+    for size in levels:
+        seg //= size
+        recvs.append(pltpu.VMEM((size - 1, seg, half), F32))
+        sums.append(pltpu.VMEM((seg, half), F32))
+    sends = sum(size - 1 for size in levels)
+    vmem = pl.BlockSpec(memory_space=pltpu.VMEM)
+    hbm = pl.BlockSpec(memory_space=pl.ANY)
+    gram, data = pl.pallas_call(
+        functools.partial(gram_kernel, levels, rows_all),
+        out_shape=(jax.ShapeDtypeStruct((n, n), F32), jax.ShapeDtypeStruct((n, rhs), F32)),
+        in_specs=[vmem, vmem],
+        out_specs=(vmem, vmem),
+        scratch_shapes=[pltpu.VMEM((length, half), F32), pltpu.VMEM((length, half), F32), *recvs, *sums]
+        + [pltpu.SemaphoreType.DMA((sends,))] * 4,
+        compiler_params=pltpu.CompilerParams(collective_id=0, has_side_effects=True, vmem_limit_bytes=40 * 2 ** 20),
+    )(jacobian, residuals)
+    return pl.pallas_call(
+        functools.partial(solve_kernel, rows_all),
+        out_shape=(jax.ShapeDtypeStruct((rows, n), F32), jax.ShapeDtypeStruct((n, n), F32), jax.ShapeDtypeStruct((n, rhs), F32)),
+        in_specs=[vmem, vmem, hbm],
+        out_specs=(hbm, vmem, vmem),
+        scratch_shapes=[pltpu.VMEM((rows, n), F32), pltpu.VMEM((rows, n), F32), pltpu.SemaphoreType.DMA, pltpu.SemaphoreType.DMA((4,))],
+        compiler_params=pltpu.CompilerParams(vmem_limit_bytes=40 * 2 ** 20),
+    )(gram, data, jacobian)
 
 
 def solution(mesh):
-    from jax.sharding import PartitionSpec as P
     return jax.shard_map(
         shards,
         mesh=mesh,

time: 128 us -> 32.6 us (0.25)
  waiting for transfers between devices: 93.5 us -> 0 us
  Pallas kernels: 9.05 us -> 29.5 us
  between operations: 14.1 us -> 0.65 us
  matrix products: 7.68 us -> 0 us
    psum x1 -> x0, waiting for transfers between devices: 93.5 us -> none  [shards(): gram, data = lax.psum((gram, data), 'row')]
    pallas_call x1 -> x2, Pallas kernels: 9.05 us -> 29.5 us  [the longest x1 18.9 us: shards(): pl.pallas_call(functools.partial(gram_kernel, levels, rows_all), out_shap...]
    dot_general x5 -> x0, matrix products: 7.68 us -> none  [dot(): lax.dot_general(a, b, (dims, ((), ())), precision=prec, preferred_element...]
    unnamed x9 -> x4, local copies, waits for them, and re-layouts: 3.43 us -> 2.26 us
  transfers between devices with their start and end apart: 1 -> 0, of which waited for: 1 -> 0; matrix products, arithmetic and copies ran while one was open for 0% -> 0% of each run, Pallas kernels for 0% -> 0%
where the time goes in v2:
time: 32.6 us; the launch traced here: 32.4 us
  Pallas kernels  29.5 us (90%)
  local copies, waits for them, and re-layouts  2.26 us (7%)
  between operations  0.65 us (2%)
    pallas_call x1, Pallas kernels, shards(): pl.pallas_call(functools.partial(gram_kernel, levels, rows_all), out_shap...  18.9 us
    pallas_call x1, Pallas kernels, shards(): pl.pallas_call(functools.partial(solve_kernel, rows_all), out_shape=(jax....  10.6 us
    unnamed x4, local copies, waits for them, and re-layouts  2.26 us

profile of v2, /device:TPU:0, one launch (start us, length us, event | category | flops | bytes accessed | tf_op | source)
XLA Modules:
  0.0 32.4 jit_solution(6387373412047466925)
XLA Ops:
  0.6 0.0 copy-start
  0.6 1.2 %copy-done = f32[1024,256]{1,0:T(8,128)S(1)} copy-done((f32[1024,256]{1,0:T(8,128)S(1)}, f32[1024,256]{1,0:T(8,128)}, u32[]{:S(2)}) %copy-start) | copy-done | bytes 1048600
  1.9 0.0 copy-start.1
  1.9 1.0 %copy-done.1 = f32[1024,128]{1,0:T(8,128)S(1)} copy-done((f32[1024,128]{1,0:T(8,128)S(1)}, f32[1024,128]{1,0:T(8,128)}, u32[]{:S(2)}) %copy-start.1) | copy-done | bytes 524312
  2.9 18.9 %shard_map.49 = (f32[256,256]{1,0:T(8,128)S(1)}, f32[256,128]{1,0:T(8,128)S(1)}) custom-call(f32[1024,256]{1,0:T(8,128)S(1)} %copy-done, f32[1024,128]{1,0:T(8,128)S(1)} %copy-done.1), custom_call_target="tpu_custom_call" | custom-call | tf_op jit(solution)/shard_map/pallas_call | solution.py:218
  21.8 10.6 %shard_map.50 = (f32[1024,256]{1,0:T(8,128)}, f32[256,256]{1,0:T(8,128)}, f32[256,128]{1,0:T(8,128)}) custom-call(f32[256,256]{1,0:T(8,128)S(1)} %get-tuple-element.5.gram_ref, f32[256,128]{1,0:T(8,128)S(1)} %get-tuple-element.6.data_ref, f32[1024,256]{1,0:T(8,128)S(1)} %copy-done), custom_call_target="tpu_custom_call" | custom-call | tf_op jit(solution)/shard_map/pallas_call | solution.py:227
Async XLA Ops:
  0.6 1.2 %copy-start = (f32[1024,256]{1,0:T(8,128)S(1)}, f32[1024,256]{1,0:T(8,128)}, u32[]{:S(2)}) copy-start(f32[1024,256]{1,0:T(8,128)} %jac_ref.3) | copy-start | bytes 3145732
  1.9 1.0 %copy-start.1 = (f32[1024,128]{1,0:T(8,128)S(1)}, f32[1024,128]{1,0:T(8,128)}, u32[]{:S(2)}) copy-start(f32[1024,128]{1,0:T(8,128)} %res_ref.1) | copy-start | bytes 1572868

commit v3 on v1

--- a/solution.py
+++ b/solution.py
@@ -1,12 +1,13 @@
-import jax, jax.numpy as jnp, functools
+import functools
+import jax
+import jax.numpy as jnp
 from jax import lax
 from jax.experimental import pallas as pl
 from jax.experimental.pallas import tpu as pltpu
+from jax.sharding import PartitionSpec as P
+
 HI = lax.Precision.HIGHEST
 F32 = jnp.float32
-
-def recip(p):
-    return 1.0 / p
 
 def factor_rows(x, extra, first, width):
     nb = x.shape[0]
@@ -25,12 +26,12 @@
         for j in range(8):
             piv = jnp.broadcast_to(cols[j][0][j:j + 1], (8, 128))
             pv = jnp.where(sub == j, piv, pv)
-            r = recip(piv)
+            r = 1.0 / piv
             f = [cj * r for cj in cols[j]]
-            f[0] = jnp.where(sub > j, f[0], 0.0)
             for l in range(j + 1, 8):
                 e = jnp.broadcast_to(cols[l][0][j:j + 1], (8, 128))
                 cols[l] = [cl - fi * e for cl, fi in zip(cols[l], f)]
+            f[0] = jnp.where(sub > j, f[0], 0.0)
             n = rows[0].shape[1]
             xr = jnp.broadcast_to(rows[p][j:j + 1], (8, n))
             er = jnp.broadcast_to(ext[p][j:j + 1], (8, 128))
@@ -48,6 +49,19 @@
 
 def dot(a, b, dims, prec=HI):
     return lax.dot_general(a, b, (dims, ((), ())), precision=prec, preferred_element_type=F32)
+
+def split3(x):
+    high = x.astype(jnp.bfloat16)
+    rest = x - high.astype(F32)
+    middle = rest.astype(jnp.bfloat16)
+    return high, middle, (rest - middle.astype(F32)).astype(jnp.bfloat16)
+
+
+def stacked_product(left, right):
+    a, b, c = split3(left)
+    d, e, f = split3(right)
+    return dot(jnp.concatenate([a, a, b, b, a, c], 0), jnp.concatenate([d, e, d, e, f, d], 0), ((0,), (0,)), None)
+
 
 def eliminate(blocks, nb):
     n = blocks[0].shape[1]
@@ -67,39 +81,209 @@
         upper.append(jnp.where(lane >= urow, x, 0.0))
         low.append(jnp.where(lane < (k + 1) * nb, t, 0.0))
         if k + 1 < count:
+            update = stacked_product(x, t)
             for i in range(k + 1, count):
-                lhs = x[:, i * nb:(i + 1) * nb]
-                upd = dot(lhs, t, ((0,), (0,)))
-                blocks[i] = jnp.where(mine, 0.0, blocks[i]) - upd
+                blocks[i] = jnp.where(mine, 0.0, blocks[i]) - update[i * nb:(i + 1) * nb]
     return upper, low
 
 
-def factor_kernel(gram_ref, upper_ref, low_ref):
+class Group:
+    def __init__(self, levels, part, total, recvs, sums, sems):
+        self.levels, self.part, self.total, self.recvs, self.sums = levels, part, total, recvs, sums
+        self.sems = sems
+        self.me = lax.axis_index("row")
+        self.places = []
+        stride = 1
+        for size in levels:
+            self.places.append((lax.rem(self.me // stride, size), stride, size))
+            stride *= size
+
+    def peer(self, level, step):
+        place, stride, size = self.places[level]
+        other = lax.rem(place + step, size)
+        return other, self.me + (other - place) * stride
+
+    def steps(self):
+        rs_send, rs_recv, ag_send, ag_recv = self.sems
+        mesh_id = pl.DeviceIdType.MESH
+        pending = []
+        source = self.part
+        slot = 0
+        for level, size in enumerate(self.levels):
+            seg = source.shape[0] // size
+            place = self.places[level][0]
+            copies = []
+            for step in range(1, size):
+                other, device = self.peer(level, step)
+                copies.append(pltpu.make_async_remote_copy(
+                    src_ref=source.at[pl.ds(pl.multiple_of(other * seg, 8), seg)],
+                    dst_ref=self.recvs[level].at[step - 1],
+                    send_sem=rs_send.at[slot], recv_sem=rs_recv.at[slot],
+                    device_id={"row": device}, device_id_type=mesh_id))
+                copies[-1].start()
+                slot += 1
+            yield
+            value = source[pl.ds(pl.multiple_of(place * seg, 8), seg)]
+            for step in range(1, size):
+                copies[step - 1].wait_recv()
+                value = value + self.recvs[level][step - 1]
+            self.sums[level][...] = value
+            pending += copies
+            source = self.sums[level]
+        starts = []
+        start = 0
+        seg = self.part.shape[0]
+        for place, _, size in self.places:
+            seg //= size
+            start = start + place * seg
+            starts.append((start, seg))
+        self.total[pl.ds(pl.multiple_of(start, 8), seg)] = source[...]
+        slot = 0
+        for level in reversed(range(len(self.levels))):
+            start, seg = starts[level]
+            mine = self.total.at[pl.ds(pl.multiple_of(start, 8), seg)]
+            copies = []
+            for step in range(1, self.levels[level]):
+                copies.append(pltpu.make_async_remote_copy(
+                    src_ref=mine, dst_ref=mine,
+                    send_sem=ag_send.at[slot], recv_sem=ag_recv.at[slot],
+                    device_id={"row": self.peer(level, step)[1]}, device_id_type=mesh_id))
+                copies[-1].start()
+                slot += 1
+            yield
+            for copy in copies:
+                copy.wait_recv()
+            pending += copies
+        for copy in pending:
+            copy.wait_send()
+
+
+def scratch_of(levels, length, width):
+    shapes = [pltpu.VMEM((length, width), F32), pltpu.VMEM((length, width), F32)]
+    recvs, sums = [], []
+    seg = length
+    for size in levels:
+        seg //= size
+        recvs.append(pltpu.VMEM((size - 1, seg, width), F32))
+        sums.append(pltpu.VMEM((seg, width), F32))
+    sends = sum(size - 1 for size in levels)
+    return shapes + recvs + sums + [pltpu.SemaphoreType.DMA((sends,))] * 4
+
+
+def group_of(levels, refs):
+    m = len(levels)
+    return Group(levels, refs[0], refs[1], refs[2:2 + m], refs[2 + m:2 + 2 * m], refs[2 + 2 * m:])
+
+
+def gram_kernel(gram_levels, rows_all, jac_ref, res_ref, gram_ref, data_ref, jac, res, in_sem, *scratch):
+    cut = 2 + 2 * len(gram_levels) + 4
+    grams = group_of(gram_levels, scratch[:cut])
+    rows, n = jac.shape
+    half = n // 2
+    chunk = rows // 4
+    loads = []
+    for i in range(4):
+        piece = pl.ds(i * chunk, chunk)
+        loads.append(pltpu.make_async_copy(jac_ref.at[piece], jac.at[piece], in_sem.at[i]))
+    loads.append(pltpu.make_async_copy(res_ref, res, in_sem.at[4]))
+    for load in loads:
+        load.start()
+
+    barrier = pltpu.get_barrier_semaphore()
+    count = 0
+    for level, size in enumerate(gram_levels):
+        for step in range(1, size):
+            pl.semaphore_signal(barrier, inc=1, device_id={"row": grams.peer(level, step)[1]}, device_id_type=pl.DeviceIdType.MESH)
+            count += 1
+
+    first = jnp.zeros((half, n), F32)
+    second = jnp.zeros((half, half), F32)
+    for i in range(4):
+        loads[i].wait()
+        panel = jac[i * chunk:(i + 1) * chunk]
+        first = first + dot(panel[:, :half], panel, ((0,), (0,)))
+        second = second + dot(panel[:, half:], panel[:, half:], ((0,), (0,)))
+    loads[4].wait()
+    data = dot(jac[...], res[...], ((0,), (0,)))
+    tiles = [first[:, :half], first[:, half:], second, data[:half], data[half:]]
+    for i, tile in enumerate(tiles):
+        grams.part[i * half:(i + 1) * half] = tile
+    if grams.part.shape[0] > 5 * half:
+        grams.part[5 * half:] = jnp.zeros((grams.part.shape[0] - 5 * half, half), F32)
+    pl.semaphore_wait(barrier, count)
+    for _ in grams.steps():
+        pass
+    total = grams.total
+    scale = 1.0 / rows_all
+    gram_ref[:half, :half] = total[:half] * scale
+    gram_ref[:half, half:] = total[half:n] * scale
+    gram_ref[half:, :half] = jnp.zeros((half, half), F32)
+    gram_ref[half:, half:] = total[n:n + half] * scale
+    data_ref[...] = total[n + half:2 * n + half]
+
+
+def solve_kernel(rows_all, gram_ref, data_ref, jac_ref, basis_ref, factor_ref, update_ref, jac, basis, factor, update, in_sem, out_sem):
+    load = pltpu.make_async_copy(jac_ref, jac, in_sem)
+    load.start()
     nb = 32
     n = gram_ref.shape[0]
     blocks = [gram_ref[i * nb:(i + 1) * nb, :] for i in range(n // nb)]
     upper, low = eliminate(blocks, nb)
     for i in range(n // nb):
-        upper_ref[i * nb:(i + 1) * nb, :] = upper[i]
-        low_ref[i * nb:(i + 1) * nb, :] = low[i]
+        factor[i * nb:(i + 1) * nb, :] = upper[i]
+    low = jnp.concatenate(low, 0)
+    load.wait()
+    pieces = 4
+    chunk = jac.shape[0] // pieces
+    stores = [pltpu.make_async_copy(factor, factor_ref, out_sem.at[pieces])]
+    stores[0].start()
+    for i in range(pieces):
+        piece = pl.ds(i * chunk, chunk)
+        basis[i * chunk:(i + 1) * chunk] = dot(jac[i * chunk:(i + 1) * chunk], low, ((1,), (1,)))
+        stores.append(pltpu.make_async_copy(basis.at[piece], basis_ref.at[piece], out_sem.at[i]))
+        stores[-1].start()
+    projected = dot(low, data_ref[...], ((1,), (0,))) * (1.0 / rows_all ** 0.5)
+    update[...] = dot(low, projected, ((0,), (0,)))
+    stores.append(pltpu.make_async_copy(update, update_ref, out_sem.at[pieces + 1]))
+    stores[-1].start()
+    for store in stores:
+        store.wait()
 
 
 def shards(jacobian, residuals):
-    rows_all = jacobian.shape[0] * lax.axis_size("row")
-    gram = dot(jacobian, jacobian, ((0,), (0,))) / rows_all
-    data = dot(jacobian, residuals, ((0,), (0,)))
-    gram, data = lax.psum((gram, data), "row")
-    shape = jax.ShapeDtypeStruct(gram.shape, F32)
-    factor, low = pl.pallas_call(factor_kernel, out_shape=(shape, shape),
-        compiler_params=pltpu.CompilerParams(vmem_limit_bytes=32 * 1024 * 1024))(gram)
-    basis = dot(jacobian, low, ((1,), (1,)))
-    projected = dot(low, data, ((1,), (0,))) / jnp.sqrt(jnp.float32(rows_all))
-    update = dot(low, projected, ((0,), (0,)))
-    return (basis, factor, update)
+    devices = lax.axis_size("row")
+    rows, n = jacobian.shape
+    rhs = residuals.shape[1]
+    half = n // 2
+    rows_all = rows * devices
+    gram_levels = (2, devices // 2)
+    unit = 8 * devices
+    gram_length = -(-5 * half // unit) * unit
+    vmem = pl.BlockSpec(memory_space=pltpu.VMEM)
+    hbm = pl.BlockSpec(memory_space=pl.ANY)
+    square = jax.ShapeDtypeStruct((n, n), F32)
+    tall = jax.ShapeDtypeStruct((n, rhs), F32)
+    gram, data = pl.pallas_call(
+        functools.partial(gram_kernel, gram_levels, rows_all),
+        out_shape=(square, tall),
+        in_specs=[hbm, hbm],
+        out_specs=(vmem, vmem),
+        scratch_shapes=[pltpu.VMEM((rows, n), F32), pltpu.VMEM((rows, rhs), F32), pltpu.SemaphoreType.DMA((5,))]
+        + scratch_of(gram_levels, gram_length, half),
+        compiler_params=pltpu.CompilerParams(collective_id=0, has_side_effects=True, vmem_limit_bytes=40 * 2 ** 20),
+    )(jacobian, residuals)
+    return pl.pallas_call(
+        functools.partial(solve_kernel, rows_all),
+        out_shape=(jax.ShapeDtypeStruct((rows, n), F32), square, tall),
+        in_specs=[vmem, vmem, hbm],
+        out_specs=(hbm, hbm, hbm),
+        scratch_shapes=[pltpu.VMEM((rows, n), F32), pltpu.VMEM((rows, n), F32), pltpu.VMEM((n, n), F32), pltpu.VMEM((n, rhs), F32),
+                        pltpu.SemaphoreType.DMA, pltpu.SemaphoreType.DMA((6,))],
+        compiler_params=pltpu.CompilerParams(vmem_limit_bytes=40 * 2 ** 20),
+    )(gram, data, jacobian)
 
 
 def solution(mesh):
-    from jax.sharding import PartitionSpec as P
     return jax.shard_map(
         shards,
         mesh=mesh,

time: 128 us -> 32.3 us (0.25)
  waiting for transfers between devices: 93.5 us -> 0 us
  Pallas kernels: 9.05 us -> 29.2 us
  between operations: 14.1 us -> 0.65 us
  matrix products: 7.68 us -> 0 us
    psum x1 -> x0, waiting for transfers between devices: 93.5 us -> none  [shards(): gram, data = lax.psum((gram, data), 'row')]
    pallas_call x1 -> x2, Pallas kernels: 9.05 us -> 29.2 us  [the longest x1 18.8 us: shards(): pl.pallas_call(functools.partial(gram_kernel, gram_levels, rows_all), out...]
    dot_general x5 -> x0, matrix products: 7.68 us -> none  [dot(): lax.dot_general(a, b, (dims, ((), ())), precision=prec, preferred_element...]
    unnamed x9 -> x4, local copies, waits for them, and re-layouts: 3.43 us -> 2.26 us
  transfers between devices with their start and end apart: 1 -> 0, of which waited for: 1 -> 0; matrix products, arithmetic and copies ran while one was open for 0% -> 0% of each run, Pallas kernels for 0% -> 0%
where the time goes in v3:
time: 32.3 us; the launch traced here: 32.1 us
  Pallas kernels  29.2 us (90%)
  local copies, waits for them, and re-layouts  2.26 us (7%)
  between operations  0.65 us (2%)
    pallas_call x1, Pallas kernels, shards(): pl.pallas_call(functools.partial(gram_kernel, gram_levels, rows_all), out...  18.8 us
    pallas_call x1, Pallas kernels, shards(): pl.pallas_call(functools.partial(solve_kernel, rows_all), out_shape=(jax....  10.4 us
    unnamed x4, local copies, waits for them, and re-layouts  2.26 us

profile of v3, /device:TPU:0, one launch (start us, length us, event | category | flops | bytes accessed | tf_op | source)
XLA Modules:
  0.0 32.1 jit_solution(10719576140517500341)
XLA Ops:
  0.6 0.0 copy-start
  0.6 1.2 %copy-done = f32[1024,256]{1,0:T(8,128)S(1)} copy-done((f32[1024,256]{1,0:T(8,128)S(1)}, f32[1024,256]{1,0:T(8,128)}, u32[]{:S(2)}) %copy-start) | copy-done | bytes 1048600
  1.9 0.0 copy-start.1
  1.9 1.0 %copy-done.1 = f32[1024,128]{1,0:T(8,128)S(1)} copy-done((f32[1024,128]{1,0:T(8,128)S(1)}, f32[1024,128]{1,0:T(8,128)}, u32[]{:S(2)}) %copy-start.1) | copy-done | bytes 524312
  2.9 18.8 %shard_map.49 = (f32[256,256]{1,0:T(8,128)S(1)}, f32[256,128]{1,0:T(8,128)S(1)}) custom-call(f32[1024,256]{1,0:T(8,128)S(1)} %copy-done, f32[1024,128]{1,0:T(8,128)S(1)} %copy-done.1), custom_call_target="tpu_custom_call" | custom-call | tf_op jit(solution)/shard_map/pallas_call | solution.py:266
  21.7 10.4 %shard_map.50 = (f32[1024,256]{1,0:T(8,128)}, f32[256,256]{1,0:T(8,128)}, f32[256,128]{1,0:T(8,128)}) custom-call(f32[256,256]{1,0:T(8,128)S(1)} %get-tuple-element.5.gram_ref, f32[256,128]{1,0:T(8,128)S(1)} %get-tuple-element.6.data_ref, f32[1024,256]{1,0:T(8,128)S(1)} %copy-done), custom_call_target="tpu_custom_call" | custom-call | tf_op jit(solution)/shard_map/pallas_call | solution.py:275
Async XLA Ops:
  0.6 1.2 %copy-start = (f32[1024,256]{1,0:T(8,128)S(1)}, f32[1024,256]{1,0:T(8,128)}, u32[]{:S(2)}) copy-start(f32[1024,256]{1,0:T(8,128)} %jac_ref.3) | copy-start | bytes 3145732
  1.9 1.0 %copy-start.1 = (f32[1024,128]{1,0:T(8,128)S(1)}, f32[1024,128]{1,0:T(8,128)}, u32[]{:S(2)}) copy-start(f32[1024,128]{1,0:T(8,128)} %res_ref.1) | copy-start | bytes 1572868
